TPU v7x, 32 devices: a whole 2x2x4 slice. The times are simulated.
32 devices in a mesh: row: 8 (over z, x), col: 4 (over y, core).
Axes of the slice: x: 2, y: 2, z: 4, core: 2. Of those that a mesh axis runs over, the one named last changes fastest.
Arguments:
- qkv: bfloat16 [3, 1408, 16384], P(None, 'col', 'row'), may hold values from -12.1 to 12.1
- residual_in: bfloat16 [1408, 16384], P('col', 'row'), may hold values from -3 to 3
- out_weight: bfloat16 [1408, 1408], replicated, may hold values from -0.625 to 0.625
- merge_weight: bfloat16 [1408, 5632], P('col'), may hold values from -0.078125 to 0.078125
- merge_gain: float32 [1408], replicated, may hold values from 0.1 to 1.9
- image_groups: int32 [32], replicated, may hold values from 1 to 256, 4096 in all
- dest_row: int32 [4096], P('row'), may hold values from 0 to 4095, as said below
Outputs:
- layer_out: bfloat16 [1408, 16384], P('col', 'row')
- image_rows: bfloat16 [1408, 4096], P('col', 'row')
Inputs may be any that keep to these rules, and one draw needn't show every extreme that they name: dest_row is a permutation of 0 to 4095. Of the 512 entries held by each index of row, exactly 64 fall in each aligned block of 512 output rows.
All inputs are finite; a program needn't handle non-finite values.
Results may differ from a plain program's by a relative error of at most 0.0064.
Values may be sent and summed in bfloat16 or wider, within the bound.
No kernel may reach another device: no remote copies, remote signals or barrier semaphores. Data moves between devices by JAX's collectives and lax.ppermute only.
A program may use at most 128 MiB of HBM per device.

v0:
```python
import math

import jax
import jax.numpy as jnp
from jax import lax
from jax.sharding import PartitionSpec as P

HEAD_DIM = 88


def with_halo(cells, sides, width):
    for axis, dim in sides:
        count = lax.axis_size(axis)
        ends = count - 1
        head = lax.slice_in_dim(cells, 0, width, axis=dim)
        tail = lax.slice_in_dim(cells, cells.shape[dim] - width, cells.shape[dim], axis=dim)
        cells = jnp.concatenate(
            [
                lax.ppermute(tail, axis, [(i, (i + 1) % count) for i in range(ends)]),
                cells,
                lax.ppermute(head, axis, [((i + 1) % count, i) for i in range(ends)]),
            ],
            axis=dim,
        )
    return cells


def image_labels(positions, image_ends, all_tokens):
    inside = (positions >= 0) & (positions < all_tokens)
    counted = jnp.sum((positions[:, None] >= image_ends[None, :]).astype(jnp.int32), axis=1)
    return jnp.where(inside, counted, -1)


def body(qkv, residual_in, out_weight, merge_weight, merge_gain, image_groups, dest_row):
    width_here = qkv.shape[1]
    tok_rows = qkv.shape[2]
    heads_here = width_here // HEAD_DIM
    full_width = out_weight.shape[0]
    reach_rows = tok_rows // 2
    block_rows = min(1024, tok_rows)
    block_count = tok_rows // block_rows
    window = block_rows + 2 * reach_rows
    row_count = lax.axis_size("row")
    row_id = lax.axis_index("row")
    col_id = lax.axis_index("col")
    all_tokens = tok_rows * row_count
    score_scale = 1.0 / math.sqrt(HEAD_DIM)
    image_ends = jnp.cumsum(image_groups) * 4
    extended = with_halo(qkv[1:], (("row", 2),), reach_rows)
    positions = (
        row_id * tok_rows - reach_rows + jnp.arange(tok_rows + 2 * reach_rows, dtype=jnp.int32)
    )
    labels = image_labels(positions, image_ends, all_tokens)

    def attend(block_id):
        first_row = block_id * block_rows
        queries = lax.dynamic_slice_in_dim(qkv[0], first_row, block_rows, 1).reshape(
            heads_here, HEAD_DIM, block_rows
        )
        key_block = lax.dynamic_slice_in_dim(extended[0], first_row, window, 1).reshape(
            heads_here, HEAD_DIM, window
        )
        value_block = lax.dynamic_slice_in_dim(extended[1], first_row, window, 1).reshape(
            heads_here, HEAD_DIM, window
        )
        query_labels = lax.dynamic_slice_in_dim(labels, first_row + reach_rows, block_rows, 0)
        key_labels = lax.dynamic_slice_in_dim(labels, first_row, window, 0)
        scores = (
            jnp.einsum("hdq,hdk->hqk", queries, key_block, preferred_element_type=jnp.float32)
            * score_scale
        )
        same_image = (query_labels[:, None] == key_labels[None, :])[None]
        scores = jnp.where(same_image, scores, -1e30)
        row_max = jnp.max(scores, axis=2, keepdims=True)
        exponent = jnp.exp(scores - row_max)
        totals = jnp.sum(exponent, axis=2)
        weights = exponent.astype(jnp.bfloat16)
        weighted = jnp.einsum(
            "hqk,hdk->hdq", weights, value_block, preferred_element_type=jnp.float32
        )
        weighted = weighted / totals[:, None, :]
        return weighted.astype(jnp.bfloat16).reshape(width_here, block_rows)

    attended = lax.map(attend, jnp.arange(block_count, dtype=jnp.int32))
    attended = jnp.transpose(attended, (1, 0, 2)).reshape(width_here, tok_rows)
    head_weight = lax.dynamic_slice_in_dim(out_weight, col_id * width_here, width_here, 0)
    partial_value = lax.dot_general(
        head_weight, attended, (((0,), (0,)), ((), ())), preferred_element_type=jnp.float32
    )
    projected = lax.psum_scatter(partial_value, "col", scatter_dimension=0, tiled=True)
    layer_out = (residual_in.astype(jnp.float32) + projected).astype(jnp.bfloat16)
    full_rows = lax.all_gather(layer_out, "col", axis=0, tiled=True)
    values32 = full_rows.astype(jnp.float32)
    centre = jnp.mean(values32, axis=0, keepdims=True)
    spread = jnp.mean(jnp.square(values32 - centre), axis=0, keepdims=True)
    normed = ((values32 - centre) * lax.rsqrt(spread + 1e-06) * merge_gain[:, None]).astype(
        jnp.bfloat16
    )
    group_rows = tok_rows // 4
    grouped = normed.reshape(full_width, group_rows, 4)
    weight_parts = merge_weight.reshape(width_here, 4, full_width)
    merged = jnp.einsum(
        "ojf,fgj->og", weight_parts, grouped, preferred_element_type=jnp.float32
    ).astype(jnp.bfloat16)
    empty_rows = jnp.zeros((width_here, group_rows), jnp.bfloat16)
    every_row, every_dest = (
        lax.all_gather(merged, "row", axis=1, tiled=True),
        lax.all_gather(dest_row, "row", axis=0, tiled=True),
    )
    slot_index = every_dest - row_id * group_rows
    slot_index = jnp.where((slot_index >= 0) & (slot_index < group_rows), slot_index, group_rows)
    image_rows = empty_rows.at[:, slot_index].set(every_row, mode="drop")
    return (layer_out, image_rows)


def solution(mesh):
    return jax.shard_map(
        body,
        mesh=mesh,
        in_specs=(P(None, "col", "row"), P("col", "row"), P(), P("col", None), P(), P(), P("row")),
        out_specs=(P("col", "row"), P("col", "row")),
        check_vma=False,
    )
```

profile of v0, /device:TPU:0, one launch (start us, length us, event | category | flops | bytes accessed | tf_op | source)
XLA Modules:
  0.0 506.4 jit_solution(16538351040245203600)
XLA Ops:
  7.2 0.0 reduce-scatter.2.cloned.1.call-start
  7.2 3.7 fusion.40
  10.9 0.0 copy-start.5
  10.9 0.0 slice-start
  10.9 6.2 %collective-permute-start = (bf16[2,352,1024]{2,1,0:T(8,128)(2,1)}, bf16[2,352,1024]{2,1,0:T(8,128)(2,1)}, u32[]{:S(2)}, u32[]{:S(2)}) collective-permute-start(bf16[2,352,1024]{2,1,0:T(8,128)(2,1)} %get-tuple-element.106), channel_id=1, source_target_pairs={{0,4},{4,8},{8,12},{12,16},{16,20},{20,24},{24,28},{1,5},{5,9},{9,... | collective-permute-start | bytes 4325384 | tf_op jit(solution)/shard_map/ppermute | solution.py:19
  17.1 1.3 collective-permute-start.1
  18.4 0.0 copy-done.5
  18.4 0.1 copy.28
  18.5 0.1 reduce-window.8
  18.6 0.1 multiply_reduce_fusion
  18.7 0.2 convert_reduce_fusion.1
  18.9 59.2 %collective-permute-done = bf16[2,352,1024]{2,1,0:T(8,128)(2,1)} collective-permute-done((bf16[2,352,1024]{2,1,0:T(8,128)(2,1)}, bf16[2,352,1024]{2,1,0:T(8,128)(2,1)}, u32[]{:S(2)}, u32[]{:S(2)}) %collective-permute-start) | collective-permute-done | bytes 1441824 | tf_op jit(solution)/shard_map/ppermute | solution.py:19
  78.0 0.0 collective-permute-done.1
  78.0 0.0 slice-done
  78.0 4.8 pad_maximum_fusion
  82.8 148.0 %while.12 = (s32[]{:T(128)}, bf16[2,352,1024]{2,1,0:T(8,128)(2,1)}, bf16[2,352,4096]{2,1,0:T(8,128)(2,1)}, s32[2]{0:T(128)S(1)}, s32[4096]{0:T(1024)S(1)}, /*ind...) while((s32[]{:T(128)}, bf16[2,352,1024]{2,1,0:T(8,128)(2,1)}, ...), condition=%wide.region_5.6_spmd, body=%wide.region_2.5_spmd.sunk | while | flops 4571455488 | bytes 204079920 | solution.py:84
  82.8 0.6 dynamic_slice.44
  84.1 2.0 broadcast_compare_fusion.2
  86.1 3.4 fusion.56
  89.5 2.4 constant_dynamic-slice_fusion.5
  91.9 1.7 slice.41
  93.6 0.1 constant_dynamic-slice_fusion.6
  93.7 0.3 copy-done
  94.0 19.4 %fusion.57 = (f32[4,1024]{1,0:T(4,128)S(1)}, f32[4,1024,3072]{2,1,0:T(8,128)}) fusion(pred[1024,3072]{1,0:T(8,128)(4,1)S(1)} %broadcast_compare_fusion.2, bf16[4,88,1024]{2,1,0:T(8,128)(2,1)S(1)} %bitcast.59, bf16[4,88,3072]{2,1,0:T(8,128)(2,1)S(1)} %bitcast.57), kind=kOutput, calls=%fused_computation.3.clone.1 | convolution fusion | flops 2252337152 | bytes 56377344 | tf_op jit(solution)/shard_map/while/body/eval_jaxpr/hdq,hdk->hqk/dot_general | solution.py:69
  113.4 22.5 %fusion.58 = f32[4,1024]{1,0:T(4,128)S(1)} fusion(f32[4,1024,3072]{2,1,0:T(8,128)} %get-tuple-element.155, f32[4,1024]{1,0:T(4,128)S(1)} %get-tuple-element.156, pred[1024,3072]{1,0:T(8,128)(4,1)S(1)} %broadcast_compare_fusion.2), kind=kLoop, calls=%fused_computation.4.clone.1 | loop fusion | flops 50327552 | bytes 53510144 | tf_op jit(solution)/shard_map/while/body/eval_jaxpr/reduce_sum | solution.py:76
  135.9 20.1 %divide_convert_fusion.2 = bf16[4,88,1024]{2,1,0:T(8,128)(2,1)S(1)} fusion(bf16[4,88,3072]{2,1,0:T(8,128)(2,1)} %bitcast.56, f32[4,1024,3072]{2,1,0:T(8,128)} %get-tuple-element.155, f32[4,1024]{1,0:T(4,128)S(1)} %get-tuple-element.156, pred[1024,3072]{1,0:T(8,128)(4,1)S(1)} %broadcast_compare_fusion.2, f32[4,1024]{1,0:T(4,128)S(1)} %fusion.58), kind=kOutput, calls=%fused_computation.9.clone.1 | convolution fusion | flops 2265645056 | bytes 56393728 | tf_op jit(solution)/shard_map/while/body/eval_jaxpr/hqk,hdk->hdq/dot_general | solution.py:78
  155.9 0.9 bitcast_dynamic-update-slice_fusion.2
  156.8 0.6 dynamic_slice.44
  158.1 2.0 broadcast_compare_fusion.2
  160.1 3.4 fusion.56
  163.5 2.4 constant_dynamic-slice_fusion.5
  165.9 1.7 slice.41
  167.6 0.1 constant_dynamic-slice_fusion.6
  167.7 0.3 copy-done
  168.0 19.4 %fusion.57 = (f32[4,1024]{1,0:T(4,128)S(1)}, f32[4,1024,3072]{2,1,0:T(8,128)}) fusion(pred[1024,3072]{1,0:T(8,128)(4,1)S(1)} %broadcast_compare_fusion.2, bf16[4,88,1024]{2,1,0:T(8,128)(2,1)S(1)} %bitcast.59, bf16[4,88,3072]{2,1,0:T(8,128)(2,1)S(1)} %bitcast.57), kind=kOutput, calls=%fused_computation.3.clone.1 | convolution fusion | flops 2252337152 | bytes 56377344 | tf_op jit(solution)/shard_map/while/body/eval_jaxpr/hdq,hdk->hqk/dot_general | solution.py:69
  187.4 22.5 %fusion.58 = f32[4,1024]{1,0:T(4,128)S(1)} fusion(f32[4,1024,3072]{2,1,0:T(8,128)} %get-tuple-element.155, f32[4,1024]{1,0:T(4,128)S(1)} %get-tuple-element.156, pred[1024,3072]{1,0:T(8,128)(4,1)S(1)} %broadcast_compare_fusion.2), kind=kLoop, calls=%fused_computation.4.clone.1 | loop fusion | flops 50327552 | bytes 53510144 | tf_op jit(solution)/shard_map/while/body/eval_jaxpr/reduce_sum | solution.py:76
  209.9 20.1 %divide_convert_fusion.2 = bf16[4,88,1024]{2,1,0:T(8,128)(2,1)S(1)} fusion(bf16[4,88,3072]{2,1,0:T(8,128)(2,1)} %bitcast.56, f32[4,1024,3072]{2,1,0:T(8,128)} %get-tuple-element.155, f32[4,1024]{1,0:T(4,128)S(1)} %get-tuple-element.156, pred[1024,3072]{1,0:T(8,128)(4,1)S(1)} %broadcast_compare_fusion.2, f32[4,1024]{1,0:T(4,128)S(1)} %fusion.58), kind=kOutput, calls=%fused_computation.9.clone.1 | convolution fusion | flops 2265645056 | bytes 56393728 | tf_op jit(solution)/shard_map/while/body/eval_jaxpr/hqk,hdk->hdq/dot_general | solution.py:78
  229.9 0.9 bitcast_dynamic-update-slice_fusion.2
  230.9 1.5 copy.36
  232.4 7.4 %fusion.34 = f32[1408,2048]{1,0:T(8,128)} fusion(bf16[352,2048]{1,0:T(8,128)(2,1)S(1)} %bitcast.60, bf16[1408,1408]{1,0:T(8,128)(2,1)} %param.11, s32[]{:T(128)S(6)} %select_n.40), kind=kOutput, calls=%fused_computation.32 | convolution fusion | flops 2030043136 | bytes 13967364 | tf_op jit(solution)/shard_map/dot_general | solution.py:87
  239.7 0.0 reduce-scatter.2.cloned.1.call-update
  239.8 0.0 all-gather.4.cloned.1.call-start
  239.8 94.5 %reduce-scatter.2.cloned.1.call-done = f32[352,2048]{1,0:T(8,128)} async-done(((f32[1408,2048]{1,0:T(8,128)}), f32[352,2048]{1,0:T(8,128)}) %reduce-scatter.2.cloned.1.call-update) | async-done | bytes 2883600 | tf_op jit(solution)/shard_map/reduce_scatter | solution.py:90
  334.3 0.0 copy-done.2
  334.3 3.3 add_convert_fusion
  337.6 0.0 all-gather.4.cloned.1.call-update
  337.7 0.0 all-gather.6.cloned.1.call-start
  337.7 43.5 %all-gather.4.cloned.1.call-done = bf16[1408,2048]{1,0:T(8,128)(2,1)} async-done(((bf16[352,2048]{1,0:T(8,128)(2,1)}), bf16[1408,2048]{1,0:T(8,128)(2,1)}) %all-gather.4.cloned.1.call-update) | async-done | bytes 5767184 | tf_op jit(solution)/shard_map/all_gather | solution.py:92
  381.2 3.7 convert_reduce_fusion
  385.0 0.0 copy-start.3
  385.0 0.6 copy-done.1
  385.5 1.5 fusion.12
  387.1 0.0 copy-done.3
  387.1 4.3 fusion.14
  391.4 8.4 %copy.30 = bf16[1408,2048]{0,1:T(8,128)(2,1)} copy(bf16[1408,2048]{1,0:T(8,128)(2,1)} %fusion.14) | data formatting | bytes 11534336 | tf_op jit(solution)/shard_map/convert_element_type | solution.py:96
  399.7 10.5 %reshape.116 = bf16[1408,512,4]{0,2,1:T(4,128)(2,1)} reshape(bf16[1408,2048]{0,1:T(8,128)(2,1)} %copy.30) | data formatting | bytes 11534336 | tf_op jit(solution)/shard_map/reshape | solution.py:100
  410.3 6.8 %fusion.29 = bf16[352,512]{1,0:T(8,128)(2,1)} fusion(bf16[1408,512,4]{0,2,1:T(4,128)(2,1)} %reshape.116, bf16[44,4,8,1408]{3,2,1,0:T(8,128)(2,1)} %bitcast.66), kind=kOutput, calls=%fused_computation.31 | convolution fusion | flops 2030223360 | bytes 10092544 | tf_op jit(solution)/shard_map/ojf,fgj->og/dot_general | solution.py:102
  417.1 0.0 all-gather.6.cloned.1.call-update
  417.1 0.0 copy-done.4
  417.1 26.4 %all-gather = s32[8,1,512]{2,1,0:T(1,128)S(1)} all-gather(s32[1,1,512]{2,1,0:T(1,128)S(1)} %bitcast.64), channel_id=1, replica_groups=mesh['row'=8,'col'=4] {'row'}, dimensions={0}, use_global_device_ids=true | all-gather | bytes 18432 | tf_op jit(solution)/shard_map/all_gather | solution.py:108
  443.5 33.9 %all-gather.6.cloned.1.call-done = bf16[352,4096]{1,0:T(8,128)(2,1)} async-done(((bf16[352,512]{1,0:T(8,128)(2,1)}), bf16[352,4096]{1,0:T(8,128)(2,1)}) %all-gather.6.cloned.1.call-update) | async-done | bytes 2883600 | tf_op jit(solution)/shard_map/all_gather | solution.py:107
  477.4 3.4 copy.33
  480.8 18.2 %scatter_custom_fusion = bf16[352,512]{0,1:T(8,128)(2,1)S(1)} fusion(s32[4096]{0:T(1024)S(1)} %compare_select_fusion, bf16[4096,352]{1,0:T(8,128)(2,1)S(1)} %copy.33, bf16[]{:T(256)} %constant.96.clone.1), kind=kCustom, calls=%fused_computation.35 | custom fusion | bytes 360450 | tf_op jit(solution)/shard_map/scatter | solution.py:112
  499.0 0.9 copy.34
  (17 shorter events, 0.1 us)
Async XLA Ops:
  7.2 327.1 %reduce-scatter.2.cloned.1.call-start = ((), (), s32[]{:S(2)}) async-start(), calls=%async_computation.1 | async-start | bytes 14417920 | tf_op jit(solution)/shard_map/reduce_scatter | solution.py:90
  10.9 7.5 %copy-start.5 = (s32[32]{0:T(128)S(1)}, s32[32]{0:T(128)}, u32[]{:S(2)}) copy-start(s32[32]{0:T(128)} %param.14) | copy-start | bytes 388
  10.9 67.1 %slice-start = ((bf16[3,352,2048]{2,1,0:T(8,128)(2,1)}), bf16[2,352,2048]{2,1,0:T(8,128)(2,1)S(1)}, s32[]{:S(2)}) async-start(bf16[3,352,2048]{2,1,0:T(8,128)(2,1)} %param.9), calls=%async_computation.4 | async-start | bytes 5767168 | tf_op jit(solution)/shard_map/slice | solution.py:49
  10.9 67.1 %collective-permute-start = (bf16[2,352,1024]{2,1,0:T(8,128)(2,1)}, bf16[2,352,1024]{2,1,0:T(8,128)(2,1)}, u32[]{:S(2)}, u32[]{:S(2)}) collective-permute-start(bf16[2,352,1024]{2,1,0:T(8,128)(2,1)} %get-tuple-element.106), channel_id=1, source_target_pairs={{0,4},{4,8},{8,12},{12,16},{16,20},{20,24},{24,28},{1,5},{5,9},{9,... | collective-permute-start | bytes 4325384 | tf_op jit(solution)/shard_map/ppermute | solution.py:19
  17.1 60.9 %collective-permute-start.1 = (bf16[2,352,1024]{2,1,0:T(8,128)(2,1)}, bf16[2,352,1024]{2,1,0:T(8,128)(2,1)}, u32[]{:S(2)}, u32[]{:S(2)}) collective-permute-start(bf16[2,352,1024]{2,1,0:T(8,128)(2,1)} %get-tuple-element.107), channel_id=1, source_target_pairs={{4,0},{8,4},{12,8},{16,12},{20,16},{24,20},{28,24},{5,1},{9,5},{13... | collective-permute-start | bytes 4325384 | tf_op jit(solution)/shard_map/ppermute | solution.py:21
  91.9 2.0 copy-start
  165.9 2.0 copy-start
  239.7 94.6 %copy-start.2 = (bf16[352,2048]{1,0:T(8,128)(2,1)S(1)}, bf16[352,2048]{1,0:T(8,128)(2,1)}, u32[]{:S(2)}) copy-start(bf16[352,2048]{1,0:T(8,128)(2,1)} %param.10) | copy-start | bytes 4325380
  239.8 141.5 %all-gather.4.cloned.1.call-start = ((), (), s32[]{:S(2)}) async-start(), calls=%async_computation.2 | async-start | bytes 7208960 | tf_op jit(solution)/shard_map/all_gather | solution.py:92
  337.7 139.8 %all-gather.6.cloned.1.call-start = ((), (), s32[]{:S(2)}) async-start(), calls=%async_computation.3 | async-start | bytes 3244032 | tf_op jit(solution)/shard_map/all_gather | solution.py:107
  381.2 4.3 copy-start.1
  385.0 2.1 copy-start.3
  410.3 6.9 %copy-start.4 = (s32[512]{0:T(512)S(1)}, s32[512]{0:T(512)}, u32[]{:S(2)}) copy-start(s32[512]{0:T(512)} %param.15) | copy-start | bytes 6148
Sparse Core Ops, SparseCore 0:
  239.9 94.3 reduce-scatter.1
  337.8 43.4 all-gather.3
  417.2 60.1 all-gather.5
where the time goes:
time: 508 us; the launch traced here: 506 us
  waiting for transfers between devices  231 us (45%)
  matrix products  93.1 us (18%)
  other arithmetic  67 us (13%)
  local copies, waits for them, and re-layouts  66 us (13%)
  blocking collectives  26.4 us (5%)
  between operations  13.9 us (3%)
  starting transfers between devices  7.61 us (1%)
    reduce_scatter x1, waiting for transfers between devices, body(): lax.psum_scatter(partial_value, 'col', scatter_dimension=0, tiled=True)  94.5 us
    ppermute x1, waiting for transfers between devices, with_halo(): lax.ppermute(tail, axis, [(i, (i + 1) % count) for i in range(ends)])  59.2 us
    reduce_sum x2, other arithmetic, attend(): totals = jnp.sum(exponent, axis=2)  45 us
    all_gather x1, waiting for transfers between devices, body(): full_rows = lax.all_gather(layer_out, 'col', axis=0, tiled=True)  43.5 us
    dot_general x2, matrix products, attend(): jnp.einsum('hqk,hdk->hdq', weights, value_block, preferred_element_type=j...  40.1 us
    dot_general x2, matrix products, attend(): jnp.einsum('hdq,hdk->hqk', queries, key_block, preferred_element_type=jnp...  38.8 us
    all_gather x1, waiting for transfers between devices, body(): lax.all_gather(merged, 'row', axis=1, tiled=True)  33.9 us
    all_gather x1, blocking collectives, body(): lax.all_gather(dest_row, 'row', axis=0, tiled=True)  26.4 us
  transfers between devices with their start and end apart: 5, of which 4 were waited for; matrix products, arithmetic and copies ran while one was open for 0% of the time, Pallas kernels for 0%

commit v1 on v0

v1 whole, which is shorter than its diff:
```python
import functools
import math

import jax
import jax.numpy as jnp
from jax import lax
from jax.experimental import pallas as pl
from jax.experimental.pallas import tpu as pltpu
from jax.sharding import PartitionSpec as P

HEAD_DIM = 88
TILE = 256
FAR = -1e30
BF = jnp.bfloat16
F32 = jnp.float32


def params(mib):
    return pltpu.CompilerParams(vmem_limit_bytes=mib * 1024 * 1024)


def cost(flops, bytes_accessed):
    return pl.CostEstimate(flops=int(flops), bytes_accessed=int(bytes_accessed), transcendentals=0)


def round_up(value, unit):
    return -(-value // unit) * unit


def key_tile(keys, label, images, depth, kt_ref):
    heads = keys.shape[0] // HEAD_DIM
    tail = depth - HEAD_DIM
    at = lax.broadcasted_iota(jnp.int32, (tail, TILE), 0)
    mask = jnp.where((at == label) | (at >= images), 0.0, FAR)
    for head in range(heads):
        whole = jnp.concatenate([keys[head * HEAD_DIM : (head + 1) * HEAD_DIM], mask], axis=0)
        kt_ref[0, head] = jnp.transpose(whole).astype(BF)


def value_tile(values, v_ref):
    heads = values.shape[0] // HEAD_DIM
    ones = jnp.where(lax.broadcasted_iota(jnp.int32, (8, TILE), 0) == 0, 1.0, 0.0)
    for head in range(heads):
        v_ref[0, head] = jnp.concatenate(
            [values[head * HEAD_DIM : (head + 1) * HEAD_DIM], ones], axis=0
        ).astype(BF)


def prepare_own(images, depth, label_ref, qkv_ref, q_ref, kt_ref, v_ref):
    label = label_ref[0]
    queries = qkv_ref[0].astype(F32)
    heads = queries.shape[0] // HEAD_DIM
    at = lax.broadcasted_iota(jnp.int32, (depth - HEAD_DIM, TILE), 0)
    mark = jnp.where(at == label, 1.0, 0.0)
    for head in range(heads):
        q_ref[0, head] = jnp.concatenate(
            [queries[head * HEAD_DIM : (head + 1) * HEAD_DIM], mark], axis=0
        ).astype(BF)
    key_tile(qkv_ref[1].astype(F32), label, images, depth, kt_ref)
    value_tile(qkv_ref[2].astype(F32), v_ref)


def prepare_halo(images, depth, label_l, label_r, left, right, kt_l, v_l, kt_r, v_r):
    key_tile(left[0].astype(F32), label_l[0], images, depth, kt_l)
    value_tile(left[1].astype(F32), v_l)
    key_tile(right[0].astype(F32), label_r[0], images, depth, kt_r)
    value_tile(right[1].astype(F32), v_r)


def reorder_residual(perm_ref, low_ref, high_ref, out_ref):
    both = jnp.concatenate([low_ref[...], high_ref[...]], axis=1)
    out_ref[0] = jnp.dot(both, perm_ref[...], preferred_element_type=F32).astype(BF)


def attend(pieces, base, rate, bounds, perm_ref, q_low, q_high, *refs):
    count = len({piece for piece, _ in pieces.values()})
    kt_refs, v_refs = refs[:count], refs[count : 2 * count]
    out_ref, kt_s, v_s, acc, top, att, kt_sem, v_sem = refs[2 * count :]
    heads = q_low.shape[1]
    first = jnp.minimum(bounds[0, 0], bounds[1, 0])
    last = jnp.maximum(bounds[0, 1], bounds[1, 1])

    def copies(tile):
        piece, at = pieces[tile]
        slot = tile - base
        return (
            pltpu.make_async_copy(kt_refs[piece].at[at], kt_s.at[slot], kt_sem.at[slot]),
            pltpu.make_async_copy(v_refs[piece].at[at], v_s.at[slot], v_sem.at[slot]),
        )

    for tile in sorted(pieces):

        @pl.when((tile >= first) & (tile < last))
        def _():
            for copy in copies(tile):
                copy.start()

    for tile in sorted(pieces):

        @pl.when((tile >= first) & (tile < last))
        def _():
            for copy in copies(tile):
                copy.wait()

    for side, q_ref in enumerate((q_low, q_high)):
        acc[...] = jnp.zeros_like(acc)
        top[...] = jnp.full_like(top, FAR)

        def step(tile, carry):
            slot = tile - base
            scores = [
                jnp.dot(kt_s[slot, head], q_ref[0, head], preferred_element_type=F32)
                for head in range(heads)
            ]
            for head in range(heads):
                before = top[head]
                now = jnp.maximum(before, jnp.max(scores[head], axis=0, keepdims=True))
                top[head] = now
                keep = jnp.exp2((before - now) * rate)
                weights = jnp.exp2((scores[head] - now) * rate).astype(BF)
                acc[head] = acc[head] * keep + jnp.dot(
                    v_s[slot, head], weights, preferred_element_type=F32
                )
            return carry

        lax.fori_loop(bounds[side, 0], bounds[side, 1], step, 0)
        whole = jnp.concatenate(
            [acc[head, :HEAD_DIM] / acc[head, HEAD_DIM : HEAD_DIM + 1] for head in range(heads)], axis=0
        )
        att[:, side * TILE : (side + 1) * TILE] = whole.astype(BF)
    out_ref[...] = jnp.dot(att[...], perm_ref[...], preferred_element_type=F32).astype(BF)


def project(order, col_ref, perm_ref, wt_ref, mw_ref, gain_ref, res_ref, *refs):
    count = len(order)
    att_refs = refs[:count]
    layer_ref, merged_ref, gathered, layer_s, normed = refs[count:]
    width = att_refs[0].shape[0]
    full = wt_ref.shape[0]
    col = col_ref[0]
    for bit, att_ref in zip(order, att_refs):
        row = pl.multiple_of((col ^ bit) * width, 16)
        gathered[pl.ds(row, width), :] = att_ref[...]
    for part in range(len(order)):
        rows = slice(part * width, (part + 1) * width)
        projected = jnp.dot(wt_ref[rows, :], gathered[...], preferred_element_type=F32)
        layer_s[rows, :] = (res_ref[part, 0].astype(F32) + projected).astype(BF)
    own = layer_s[pl.ds(pl.multiple_of(col * width, 16), width), :]
    layer_ref[...] = lax.dot_general(
        own, perm_ref[...], (((1,), (1,)), ((), ())), preferred_element_type=F32
    ).astype(BF)
    values = layer_s[...].astype(F32)
    centre = jnp.mean(values, axis=0, keepdims=True)
    spread = jnp.mean(jnp.square(values - centre), axis=0, keepdims=True)
    normed[...] = ((values - centre) * lax.rsqrt(spread + 1e-06) * gain_ref[...]).astype(BF)
    groups = normed.shape[1] // 4
    total = jnp.zeros((width, groups), F32)
    for j in range(4):
        total += jnp.dot(
            mw_ref[:, j * full : (j + 1) * full],
            normed[:, j * groups : (j + 1) * groups],
            preferred_element_type=F32,
        )
    merged_ref[...] = total.astype(BF)


def outgoing(slot_ref, place_ref, *refs):
    out_ref = refs[-1]
    total = None
    slots = out_ref.shape[0]
    for stage, merged_ref in enumerate(refs[:-1]):
        groups = merged_ref.shape[1]
        row = lax.broadcasted_iota(jnp.int32, (slots, groups), 0)
        pick = jnp.where(row == slot_ref[stage], 1.0, 0.0).astype(BF)
        rows = jnp.concatenate([merged_ref[...], place_ref[stage]], axis=0)
        term = lax.dot_general(pick, rows, (((1,), (1,)), ((), ())), preferred_element_type=F32)
        total = term if total is None else total + term
    out_ref[...] = total.astype(BF)


def incoming(width, base, in_ref, out_ref):
    place = in_ref[:, width : width + 2].astype(F32)
    target = (place[:, 0:1] * base + place[:, 1:2]).astype(jnp.int32)
    slots = in_ref.shape[0]
    lane = lax.broadcasted_iota(jnp.int32, (slots, slots), 1)
    pick = jnp.where(lane == target, 1.0, 0.0).astype(BF)
    out_ref[...] = lax.dot_general(
        in_ref[:, :width], pick, (((0,), (0,)), ((), ())), preferred_element_type=F32
    ).astype(BF)


def body(qkv, residual_in, out_weight, merge_weight, merge_gain, image_groups, dest_row):
    width = qkv.shape[1]
    tokens = qkv.shape[2]
    heads = width // HEAD_DIM
    full = out_weight.shape[0]
    images = image_groups.shape[0]
    reach = tokens // 2
    own_tiles = tokens // TILE
    far_tiles = reach // TILE
    stages = own_tiles // 2
    depth = round_up(HEAD_DIM + images, 128)
    rate = math.log2(math.e) / math.sqrt(HEAD_DIM)
    rows, cols = lax.axis_size("row"), lax.axis_size("col")
    row_id, col_id = lax.axis_index("row"), lax.axis_index("col")
    forward = [(i, i + 1) for i in range(rows - 1)]
    backward = [(i + 1, i) for i in range(rows - 1)]

    lefts, rights = [], []
    for stage in range(far_tiles):
        tail = lax.slice_in_dim(qkv[1:], tokens - (stage + 1) * TILE, tokens - stage * TILE, axis=2)
        head = lax.slice_in_dim(qkv[1:], stage * TILE, (stage + 1) * TILE, axis=2)
        lefts.append(lax.ppermute(tail, "row", forward))
        rights.append(lax.ppermute(head, "row", backward))

    image_ends = jnp.cumsum(image_groups) * 4
    window_tiles = own_tiles + 2 * far_tiles
    positions = row_id * tokens - reach + jnp.arange(window_tiles * TILE, dtype=jnp.int32)
    labels = jnp.sum((positions[:, None] >= image_ends[None, :]).astype(jnp.int32), axis=1)
    labels = jnp.where(positions >= 0, labels, -1).reshape(window_tiles, 1, TILE)
    starts = row_id * tokens + jnp.arange(own_tiles, dtype=jnp.int32) * TILE
    ends = starts + TILE - 1
    low = jnp.max(jnp.where(image_ends[None, :] <= starts[:, None], image_ends[None, :], 0), axis=1)
    high = jnp.min(
        jnp.where(image_ends[None, :] > ends[:, None], image_ends[None, :], rows * tokens), axis=1
    )
    window_start = row_id * tokens - reach
    low = (low - window_start) // TILE
    high = (high - window_start + TILE - 1) // TILE
    tile_at = jnp.arange(own_tiles, dtype=jnp.int32)
    low = jnp.maximum(low, tile_at)
    high = jnp.minimum(high, tile_at + 2 * far_tiles + 1)

    at = jnp.arange(2 * TILE, dtype=jnp.int32)
    perm = (((at % 4) * (TILE // 2) + at // 4)[:, None] == at[None, :]).astype(BF)

    residual = pl.pallas_call(
        reorder_residual,
        grid=(stages,),
        in_specs=[
            pl.BlockSpec((2 * TILE, 2 * TILE), lambda i: (0, 0)),
            pl.BlockSpec((width, TILE), lambda i: (0, stages - 1 - i)),
            pl.BlockSpec((width, TILE), lambda i: (0, stages + i)),
        ],
        out_specs=pl.BlockSpec((1, width, 2 * TILE), lambda i: (i, 0, 0)),
        out_shape=jax.ShapeDtypeStruct((stages, width, 2 * TILE), BF),
        compiler_params=params(32),
        cost_estimate=cost(2 * width * tokens * 2 * TILE, 4 * width * tokens),
        name="reorder_residual",
    )(perm, residual_in, residual_in)
    residual = lax.all_gather(residual, "col", axis=0)

    kt_shape, v_shape = (heads, TILE, depth), (heads, HEAD_DIM + 8, TILE)
    label_spec = lambda tile: pl.BlockSpec((1, 1, TILE), lambda i: (tile, 0, 0))
    q_tiles, kt_own, v_own = pl.pallas_call(
        functools.partial(prepare_own, images, depth),
        grid=(own_tiles,),
        in_specs=[
            pl.BlockSpec((1, 1, TILE), lambda i: (i + far_tiles, 0, 0)),
            pl.BlockSpec((3, width, TILE), lambda i: (0, 0, i)),
        ],
        out_specs=[
            pl.BlockSpec((1, heads, depth, TILE), lambda i: (i, 0, 0, 0)),
            pl.BlockSpec((1,) + kt_shape, lambda i: (i, 0, 0, 0)),
            pl.BlockSpec((1,) + v_shape, lambda i: (i, 0, 0, 0)),
        ],
        out_shape=[
            jax.ShapeDtypeStruct((own_tiles, heads, depth, TILE), BF),
            jax.ShapeDtypeStruct((own_tiles,) + kt_shape, BF),
            jax.ShapeDtypeStruct((own_tiles,) + v_shape, BF),
        ],
        compiler_params=params(32),
        cost_estimate=cost(2e9, 16 * width * tokens),
        name="prepare_own",
    )(labels, qkv)

    out_weight_t = jnp.transpose(out_weight)
    gain = merge_gain[:, None]
    bits = []
    span = cols // 2
    while span:
        bits.append(span)
        span //= 2
    order = [0]
    for bit in bits:
        order = order + [bit ^ other for other in order]
    col_value = col_id.astype(jnp.int32).reshape(1)

    halo = []
    layers, merged = [], []
    any_spec = pl.BlockSpec(memory_space=pl.ANY)
    smem_spec = pl.BlockSpec(memory_space=pltpu.SMEM)
    vmem_spec = pl.BlockSpec(memory_space=pltpu.VMEM)
    for stage in range(stages):
        left_tile, right_tile = far_tiles - 1 - stage, far_tiles + own_tiles + stage
        chunk_spec = pl.BlockSpec((2, width, TILE), lambda i: (0, 0, 0))
        new = pl.pallas_call(
            functools.partial(prepare_halo, images, depth),
            grid=(1,),
            in_specs=[label_spec(left_tile), label_spec(right_tile), chunk_spec, chunk_spec],
            out_specs=[
                pl.BlockSpec((1,) + kt_shape, lambda i: (0, 0, 0, 0)),
                pl.BlockSpec((1,) + v_shape, lambda i: (0, 0, 0, 0)),
            ]
            * 2,
            out_shape=[
                jax.ShapeDtypeStruct((1,) + kt_shape, BF),
                jax.ShapeDtypeStruct((1,) + v_shape, BF),
            ]
            * 2,
            compiler_params=params(32),
            cost_estimate=cost(5e8, 16 * width * TILE),
            name="prepare_halo",
        )(labels, labels, lefts[stage], rights[stage])
        halo.append(new)

        pieces = {far_tiles + t: (0, t) for t in range(own_tiles)}
        kts, vs = [kt_own], [v_own]
        for before in range(stage + 1):
            for tile, at_piece in (
                (far_tiles - 1 - before, 0),
                (far_tiles + own_tiles + before, 2),
            ):
                pieces[tile] = (len(kts), 0)
                kts.append(halo[before][at_piece])
                vs.append(halo[before][at_piece + 1])
        tiles = len(pieces)
        low_tile, high_tile = stages - 1 - stage, stages + stage
        bounds = jnp.stack(
            [
                jnp.stack([low[low_tile], high[low_tile]]),
                jnp.stack([low[high_tile], high[high_tile]]),
            ]
        )
        q_spec = lambda tile: pl.BlockSpec((1, heads, depth, TILE), lambda i: (tile, 0, 0, 0))
        attended = pl.pallas_call(
            functools.partial(attend, pieces, min(pieces), rate),
            grid=(1,),
            in_specs=[smem_spec, vmem_spec, q_spec(low_tile), q_spec(high_tile)]
            + [any_spec] * (2 * len(kts)),
            out_specs=vmem_spec,
            out_shape=jax.ShapeDtypeStruct((width, 2 * TILE), BF),
            scratch_shapes=[
                pltpu.VMEM((tiles,) + kt_shape, BF),
                pltpu.VMEM((tiles,) + v_shape, BF),
                pltpu.VMEM((heads, HEAD_DIM + 8, TILE), F32),
                pltpu.VMEM((heads, 1, TILE), F32),
                pltpu.VMEM((width, 2 * TILE), BF),
                pltpu.SemaphoreType.DMA((tiles,)),
                pltpu.SemaphoreType.DMA((tiles,)),
            ],
            compiler_params=params(48),
            cost_estimate=cost(4e9, 4e6),
            name="attend",
        )(bounds, perm, q_tiles, q_tiles, *kts, *vs)

        gathered = [attended]
        for bit in bits:
            pairs = [(i, i ^ bit) for i in range(cols)]
            gathered = gathered + [lax.ppermute(piece, "col", pairs) for piece in gathered]

        layer, part = pl.pallas_call(
            functools.partial(project, order),
            grid=(1,),
            in_specs=[
                smem_spec,
                vmem_spec,
                vmem_spec,
                vmem_spec,
                vmem_spec,
                pl.BlockSpec((cols, 1, width, 2 * TILE), functools.partial(lambda s, i: (0, s, 0, 0), stage)),
            ]
            + [vmem_spec] * cols,
            out_specs=[vmem_spec, vmem_spec],
            out_shape=[
                jax.ShapeDtypeStruct((width, 2 * TILE), BF),
                jax.ShapeDtypeStruct((width, TILE // 2), BF),
            ],
            scratch_shapes=[
                pltpu.VMEM((full, 2 * TILE), BF),
                pltpu.VMEM((full, 2 * TILE), BF),
                pltpu.VMEM((full, 2 * TILE), BF),
            ],
            compiler_params=params(48),
            cost_estimate=cost(2 * full * full * 2 * TILE + 2 * width * full * 2 * TILE, 10e6),
            name="project",
        )(col_value, perm, out_weight_t, merge_weight, gain, residual, *gathered)
        layers.append(layer)
        merged.append(part)

    layer_out = jnp.concatenate(
        [layers[s][:, :TILE] for s in reversed(range(stages))]
        + [layers[s][:, TILE:] for s in range(stages)],
        axis=1,
    )

    groups = tokens // 4
    share = groups // rows
    piece_groups = TILE // 4
    owner = dest_row // groups
    place = dest_row % groups
    index = jnp.arange(groups, dtype=jnp.int32)
    rank = jnp.sum(
        ((owner[:, None] == owner[None, :]) & (index[None, :] < index[:, None])).astype(jnp.int32),
        axis=1,
    )
    base = 32
    info = jnp.stack([owner * share + rank, place // base, place % base])
    info = info.reshape(3, own_tiles, piece_groups)
    info = jnp.stack(
        [
            jnp.concatenate([info[:, stages - 1 - s], info[:, stages + s]], axis=1)
            for s in range(stages)
        ],
        axis=1,
    )
    slots = info[0][:, None, :]
    wide = round_up(width + 2, 128)
    places = jnp.concatenate(
        [
            jnp.stack([info[1], info[2]], axis=1).astype(BF),
            jnp.zeros((stages, wide - width - 2, 2 * piece_groups), BF),
        ],
        axis=1,
    )
    sent = pl.pallas_call(
        outgoing,
        out_shape=jax.ShapeDtypeStruct((groups, wide), BF),
        compiler_params=params(32),
        cost_estimate=cost(2 * groups * groups * wide, 2e6),
        name="outgoing",
    )(slots, places, *merged)
    received = lax.all_to_all(
        sent.reshape(rows, share, wide), "row", split_axis=0, concat_axis=0, tiled=True
    ).reshape(groups, wide)
    image_rows = pl.pallas_call(
        functools.partial(incoming, width, base),
        out_shape=jax.ShapeDtypeStruct((width, groups), BF),
        compiler_params=params(32),
        cost_estimate=cost(2 * groups * groups * wide, 2e6),
        name="incoming",
    )(received)
    return (layer_out, image_rows)


def solution(mesh):
    return jax.shard_map(
        body,
        mesh=mesh,
        in_specs=(P(None, "col", "row"), P("col", "row"), P(), P("col", None), P(), P(), P("row")),
        out_specs=(P("col", "row"), P("col", "row")),
        check_vma=False,
    )
```

time: 508 us -> 190 us (0.37)
  waiting for transfers between devices: 231 us -> 16.3 us
  matrix products: 93.1 us -> 0 us
  Pallas kernels: 0 us -> 82.8 us
  other arithmetic: 67 us -> 11.9 us
  local copies, waits for them, and re-layouts: 66 us -> 22.1 us
  starting transfers between devices: 7.61 us -> 42.9 us
  blocking collectives: 26.4 us -> 0 us
    reduce_scatter x1 -> x0, waiting for transfers between devices: 94.5 us -> none  [body(): lax.psum_scatter(partial_value, 'col', scatter_dimension=0, tiled=True)]
    dot_general x6 -> x0, matrix products: 93.1 us -> none  [the longest x2 40.1 us: attend(): jnp.einsum('hqk,hdk->hdq', weights, value_block, preferred_element_type=j...]
    pallas_call x0 -> x16, Pallas kernels: none -> 82.8 us  [the longest x4 41.2 us: body(): pl.pallas_call(functools.partial(attend, pieces, min(pieces), rate), grid...]
    all_gather x2 -> x1, waiting for transfers between devices: 77.4 us -> 0.01 us  [body(): residual = lax.all_gather(residual, 'col', axis=0)]
    ppermute x2 -> x20, waiting for transfers between devices: 59.2 us -> 8.92 us  [the longest x4 8.87 us: body(): lefts.append(lax.ppermute(tail, 'row', forward))]
    reduce_sum x5 -> x2, other arithmetic: 50.5 us -> 0.4 us  [the longest x1 0.25 us: body(): jnp.sum(((owner[:, None] == owner[None, :]) & (index[None, :] < index[:,...]
    all_gather x1 -> x0, blocking collectives: 26.4 us -> none  [body(): lax.all_gather(dest_row, 'row', axis=0, tiled=True)]
    ppermute x2 -> x20, starting transfers between devices: 7.49 us -> 31.4 us  [the longest x4 20.4 us: body(): lefts.append(lax.ppermute(tail, 'row', forward))]
  transfers between devices with their start and end apart: 5 -> 22, of which waited for: 4 -> 2; matrix products, arithmetic and copies ran while one was open for 0% -> 15% of each run, Pallas kernels for 0% -> 36%
where the time goes in v1:
time: 190 us
  Pallas kernels  82.8 us (44%)
  starting transfers between devices  42.9 us (23%)
  local copies, waits for them, and re-layouts  22.1 us (12%)
  waiting for transfers between devices  16.3 us (9%)
  between operations  14.5 us (8%)
  other arithmetic  11.9 us (6%)
    pallas_call x4, Pallas kernels, body(): pl.pallas_call(functools.partial(attend, pieces, min(pieces), rate), grid...  41.2 us
    pallas_call x4, Pallas kernels, body(): pl.pallas_call(functools.partial(project, order), grid=(1,), in_specs=[sm...  33.5 us
    ppermute x4, starting transfers between devices, body(): lefts.append(lax.ppermute(tail, 'row', forward))  20.4 us
    unnamed x27, local copies, waits for them, and re-layouts  16.4 us
    all_to_all x1, starting transfers between devices, body(): lax.all_to_all(sent.reshape(rows, share, wide), 'row', split_axis=0, conc...  11.4 us
    another operation x12, other arithmetic, body(): jnp.stack([jnp.stack([low[low_tile], high[low_tile]]), jnp.stack([low[hig...  10.6 us
    ppermute x4, waiting for transfers between devices, body(): lefts.append(lax.ppermute(tail, 'row', forward))  8.87 us
    all_to_all x1, waiting for transfers between devices, body(): lax.all_to_all(sent.reshape(rows, share, wide), 'row', split_axis=0, conc...  7.33 us
  transfers between devices with their start and end apart: 22, of which 2 were waited for; matrix products, arithmetic and copies ran while one was open for 15% of the time, Pallas kernels for 36%

profile of v1, /device:TPU:0, one launch (start us, length us, event | category | flops | bytes accessed | tf_op | source)
XLA Modules:
  0.0 190.4 jit_solution(16433034833999921944)
XLA Ops:
  7.2 0.2 fusion.perm_ref
  7.4 1.4 copy-done
  8.7 2.7 %reorder_residual.1 = bf16[4,352,512]{2,1,0:T(8,128)(2,1)} custom-call(bf16[512,512]{1,0:T(8,128)(2,1)S(1)} %fusion.perm_ref, bf16[352,2048]{1,0:T(8,128)(2,1)S(1)} %copy-done, bf16[352,2048]{1,0:T(8,128)(2,1)S(1)} %copy-done), custom_call_target="tpu_custom_call" | custom-call | flops 738197504 | bytes 2883584 | tf_op jit(solution)/shard_map/reorder_residual/pallas_call | solution.py:237
  11.5 3.0 %fusion.17 = (bf16[2,352,256]{2,1,0:T(8,128)(2,1)}, bf16[2,352,256]{2,1,0:T(8,128)(2,1)}, bf16[2,352,256]{2,1,0:T(8,128)(2,1)S(1)}, bf16[2,352,256]{2,1,0:T(8,12...) fusion(bf16[3,352,2048]{2,1,0:T(8,128)(2,1)} %qkv_ref.1), kind=kLoop, calls=%fused_computation.93 | loop fusion | bytes 5767168 | tf_op jit(solution)/shard_map/slice | solution.py:212
  14.5 1.3 collective-permute-start.7
  15.8 1.3 collective-permute-start.5
  17.1 6.1 %collective-permute-start.4 = (bf16[2,352,256]{2,1,0:T(8,128)(2,1)S(1)}, bf16[2,352,256]{2,1,0:T(8,128)(2,1)S(1)}, u32[]{:S(2)}, u32[]{:S(2)}) collective-permute-start(bf16[2,352,256]{2,1,0:T(8,128)(2,1)S(1)} %get-tuple-element.62), channel_id=1, source_target_pairs={{0,4},{4,8},{8,12},{12,16},{16,20},{20,24},{24,28},{1,5},{5,9},{9,... | collective-permute-start | bytes 1081352 | tf_op jit(solution)/shard_map/ppermute | solution.py:213
  23.2 1.3 collective-permute-start.1
  24.5 5.4 %collective-permute-start = (bf16[2,352,256]{2,1,0:T(8,128)(2,1)}, bf16[2,352,256]{2,1,0:T(8,128)(2,1)S(1)}, u32[]{:S(2)}, u32[]{:S(2)}) collective-permute-start(bf16[2,352,256]{2,1,0:T(8,128)(2,1)} %get-tuple-element.66), channel_id=1, source_target_pairs={{0,4},{4,8},{8,12},{12,16},{16,20},{20,24},{24,28},{1,5},{5,9},{9,... | collective-permute-start | bytes 1081352 | tf_op jit(solution)/shard_map/ppermute | solution.py:213
  30.1 0.2 convert_reduce_fusion
  31.1 0.2 select_reduce_fusion.1
  31.3 0.7 fusion.19
  32.0 0.7 fusion.18
  32.7 1.3 add_bitcast_fusion.9
  34.1 1.3 add_bitcast_fusion.10
  35.4 1.3 add_bitcast_fusion.8
  36.7 1.3 add_bitcast_fusion.7
  38.0 1.3 add_bitcast_fusion.6
  39.2 1.3 add_bitcast_fusion.5
  40.5 1.4 add_bitcast_fusion.4
  41.9 1.4 add_bitcast_fusion.3
  43.6 2.2 %copy-done.1 = bf16[3,352,2048]{2,1,0:T(8,128)(2,1)S(1)} copy-done((bf16[3,352,2048]{2,1,0:T(8,128)(2,1)S(1)}, bf16[3,352,2048]{2,1,0:T(8,128)(2,1)}, u32[]{:S(2)}) %copy-start.1) | copy-done | bytes 4325400
  45.8 1.8 prepare_own.1
  47.6 1.3 copy-done.5
  49.0 1.3 collective-permute-start.3
  50.3 8.9 %collective-permute-done.left = bf16[2,352,256]{2,1,0:T(8,128)(2,1)S(1)} collective-permute-done((bf16[2,352,256]{2,1,0:T(8,128)(2,1)}, bf16[2,352,256]{2,1,0:T(8,128)(2,1)S(1)}, u32[]{:S(2)}, u32[]{:S(2)}) %collective-permute-start) | collective-permute-done | bytes 360480 | tf_op jit(solution)/shard_map/ppermute | solution.py:213
  59.1 4.3 %collective-permute-start.2 = (bf16[2,352,256]{2,1,0:T(8,128)(2,1)S(1)}, bf16[2,352,256]{2,1,0:T(8,128)(2,1)S(1)}, u32[]{:S(2)}, u32[]{:S(2)}) collective-permute-start(bf16[2,352,256]{2,1,0:T(8,128)(2,1)S(1)} %get-tuple-element.64), channel_id=1, source_target_pairs={{0,4},{4,8},{8,12},{12,16},{16,20},{20,24},{24,28},{1,5},{5,9},{9,... | collective-permute-start | bytes 1081352 | tf_op jit(solution)/shard_map/ppermute | solution.py:213
  63.4 0.2 prepare_halo.4
  63.6 8.9 %attend.7.refs_0_ = bf16[352,512]{1,0:T(8,128)(2,1)S(1)} custom-call(s32[2,2]{1,0:T(2,128)S(1)} %pad_add_fusion.6.bounds, bf16[512,512]{1,0:T(8,128)(2,1)S(1)} %fusion.perm_ref, bf16[8,4,128,256]{3,2,1,0:T(8,128)(2,1)S(1)} %get-tuple-element.29.q_low.q_high, bf16[8,4,128,256]{3,2,1,0:T(8,128)(2,1)S(1)} %get-tuple-element.29.q_low.q_high, ...), custom_call_target="tpu_custom_call" | custom-call | flops 4000000000 | bytes 4000000 | tf_op jit(solution)/shard_map/attend/pallas_call | solution.py:336
  72.6 4.5 %collective-permute-start.6 = (bf16[2,352,256]{2,1,0:T(8,128)(2,1)}, bf16[2,352,256]{2,1,0:T(8,128)(2,1)S(1)}, u32[]{:S(2)}, u32[]{:S(2)}) collective-permute-start(bf16[2,352,256]{2,1,0:T(8,128)(2,1)} %get-tuple-element.67), channel_id=1, source_target_pairs={{0,4},{4,8},{8,12},{12,16},{16,20},{20,24},{24,28},{1,5},{5,9},{9,... | collective-permute-start | bytes 1081352 | tf_op jit(solution)/shard_map/ppermute | solution.py:213
  77.2 0.2 prepare_halo.5
  77.4 12.2 %attend.6.refs_0_ = bf16[352,512]{1,0:T(8,128)(2,1)S(1)} custom-call(s32[2,2]{1,0:T(2,128)S(1)} %pad_add_fusion.5.bounds, bf16[512,512]{1,0:T(8,128)(2,1)S(1)} %fusion.perm_ref, bf16[8,4,128,256]{3,2,1,0:T(8,128)(2,1)} %copy-done.4, bf16[8,4,128,256]{3,2,1,0:T(8,128)(2,1)} %copy-done.4, bf16[8,4,256,128]{3,2,1,0:T(8,128)(2,1)} %copy-done.5, ...), custom_call_target="tpu_custom_call" | custom-call | flops 4000000000 | bytes 4000000 | tf_op jit(solution)/shard_map/attend/pallas_call | solution.py:336
  89.6 1.6 collective-permute-start.17
  91.2 0.2 collective-permute-start.15
  91.4 0.2 prepare_halo.6
  91.6 10.8 %attend.5.refs_0_ = bf16[352,512]{1,0:T(8,128)(2,1)S(1)} custom-call(s32[2,2]{1,0:T(2,128)S(1)} %pad_add_fusion.4.bounds, bf16[512,512]{1,0:T(8,128)(2,1)S(1)} %fusion.perm_ref, bf16[8,4,128,256]{3,2,1,0:T(8,128)(2,1)} %copy-done.4, bf16[8,4,128,256]{3,2,1,0:T(8,128)(2,1)} %copy-done.4, bf16[8,4,256,128]{3,2,1,0:T(8,128)(2,1)} %copy-done.5, ...), custom_call_target="tpu_custom_call" | custom-call | flops 4000000000 | bytes 4000000 | tf_op jit(solution)/shard_map/attend/pallas_call | solution.py:336
  102.4 0.6 collective-permute-start.14
  103.0 1.5 collective-permute-start.11
  104.5 0.2 prepare_halo.7
  104.9 9.4 %attend.4.refs_0_ = bf16[352,512]{1,0:T(8,128)(2,1)} custom-call(s32[2,2]{1,0:T(2,128)S(1)} %pad_add_fusion.3.bounds, bf16[512,512]{1,0:T(8,128)(2,1)S(1)} %fusion.perm_ref, bf16[8,4,128,256]{3,2,1,0:T(8,128)(2,1)} %copy-done.4, bf16[8,4,128,256]{3,2,1,0:T(8,128)(2,1)} %copy-done.4, bf16[8,4,256,128]{3,2,1,0:T(8,128)(2,1)} %copy-done.5, ...), custom_call_target="tpu_custom_call" | custom-call | flops 4000000000 | bytes 4000000 | tf_op jit(solution)/shard_map/attend/pallas_call | solution.py:336
  114.2 0.6 collective-permute-start.8
  114.8 0.2 collective-permute-start.16
  115.0 0.2 broadcast_in_dim.42.gain_ref
  115.3 6.3 %copy.49 = bf16[1408,1408]{0,1:T(8,128)(2,1)} copy(bf16[1408,1408]{1,0:T(8,128)(2,1)} %param.9) | data formatting | bytes 7929856 | tf_op args[2]
  121.6 0.4 collective-permute-start.12
  122.0 0.2 collective-permute-start.13
  122.1 1.0 copy-done.3
  123.1 8.2 %project.7 = (bf16[352,512]{1,0:T(8,128)(2,1)S(1)}, bf16[352,128]{1,0:T(8,128)(2,1)S(1)}) custom-call(s32[1]{0:T(128)} %bitcast.col_ref, bf16[512,512]{1,0:T(8,128)(2,1)S(1)} %fusion.perm_ref, bf16[1408,1408]{1,0:T(8,128)(2,1)} %bitcast.52, bf16[352,5632]{1,0:T(8,128)(2,1)} %mw_ref.7, f32[1408,1]{1,0:T(8,128)S(1)} %broadcast_in_dim.42.gain_ref, ...), custom_call_target="tpu_custom_call" | custom-call | flops 2537553920 | bytes 10000000 | tf_op jit(solution)/shard_map/project/pallas_call | solution.py:362
  131.4 0.4 collective-permute-start.9
  131.8 0.2 collective-permute-start.10
  132.0 8.4 %project.6 = (bf16[352,512]{1,0:T(8,128)(2,1)S(1)}, bf16[352,128]{1,0:T(8,128)(2,1)S(1)}) custom-call(s32[1]{0:T(128)} %bitcast.col_ref, bf16[512,512]{1,0:T(8,128)(2,1)S(1)} %fusion.perm_ref, bf16[1408,1408]{1,0:T(8,128)(2,1)} %bitcast.53, bf16[352,5632]{1,0:T(8,128)(2,1)} %mw_ref.7, f32[1408,1]{1,0:T(8,128)S(1)} %broadcast_in_dim.42.gain_ref, ...), custom_call_target="tpu_custom_call" | custom-call | flops 2537553920 | bytes 10000000 | tf_op jit(solution)/shard_map/project/pallas_call | solution.py:362
  140.4 8.4 %project.5 = (bf16[352,512]{1,0:T(8,128)(2,1)S(1)}, bf16[352,128]{1,0:T(8,128)(2,1)S(1)}) custom-call(s32[1]{0:T(128)} %bitcast.col_ref, bf16[512,512]{1,0:T(8,128)(2,1)S(1)} %fusion.perm_ref, bf16[1408,1408]{1,0:T(8,128)(2,1)} %bitcast.54, bf16[352,5632]{1,0:T(8,128)(2,1)} %mw_ref.7, f32[1408,1]{1,0:T(8,128)S(1)} %broadcast_in_dim.42.gain_ref, ...), custom_call_target="tpu_custom_call" | custom-call | flops 2537553920 | bytes 10000000 | tf_op jit(solution)/shard_map/project/pallas_call | solution.py:362
  148.8 8.5 %project.4 = (bf16[352,512]{1,0:T(8,128)(2,1)S(1)}, bf16[352,128]{1,0:T(8,128)(2,1)S(1)}) custom-call(s32[1]{0:T(128)} %bitcast.col_ref, bf16[512,512]{1,0:T(8,128)(2,1)S(1)} %fusion.perm_ref, bf16[1408,1408]{1,0:T(8,128)(2,1)} %bitcast.55, bf16[352,5632]{1,0:T(8,128)(2,1)} %mw_ref.7, f32[1408,1]{1,0:T(8,128)S(1)} %broadcast_in_dim.42.gain_ref, ...), custom_call_target="tpu_custom_call" | custom-call | flops 2537553920 | bytes 10000000 | tf_op jit(solution)/shard_map/project/pallas_call | solution.py:362
  157.3 1.3 outgoing.1
  158.7 11.4 %all-to-all-start = ((bf16[8,64,384]{2,1,0:T(8,128)(2,1)}), bf16[8,64,384]{2,1,0:T(8,128)(2,1)S(1)}, u32[]{:S(2)}, u32[]{:S(2)}) async-start(bf16[8,64,384]{2,1,0:T(8,128)(2,1)} %bitcast.27), calls=%async_computation | async-start | bytes 786432 | tf_op jit(solution)/shard_map/all_to_all | solution.py:433
  170.1 0.7 slice_dynamic-update-slice_fusion.5
  170.7 0.7 slice_dynamic-update-slice_fusion.4
  171.4 0.7 slice_dynamic-update-slice_fusion.3
  172.1 0.8 constant_dynamic-update-slice_fusion
  172.9 0.7 slice_dynamic-update-slice_fusion.2
  173.5 0.7 slice_dynamic-update-slice_fusion.1
  174.2 0.7 slice_dynamic-update-slice_fusion
  174.9 7.3 %all-to-all-done = bf16[8,64,384]{2,1,0:T(8,128)(2,1)S(1)} async-done(((bf16[8,64,384]{2,1,0:T(8,128)(2,1)}), bf16[8,64,384]{2,1,0:T(8,128)(2,1)S(1)}, u32[]{:S(2)}, u32[]{:S(2)}) %all-to-all-start) | async-done | bytes 393248 | tf_op jit(solution)/shard_map/all_to_all | solution.py:433
  182.2 1.3 incoming.1
  (74 shorter events, 1.4 us)
Async XLA Ops:
  7.2 115.0 %all-gather.3.cloned.1.call-start = ((), (), s32[]{:S(2)}) async-start(), calls=%async_computation.1 | async-start | bytes 7208960 | tf_op jit(solution)/shard_map/all_gather | solution.py:251
  7.4 1.4 copy-start
  11.5 18.5 %copy-start.8 = (s32[512]{0:T(512)S(1)}, s32[512]{0:T(512)}, u32[]{:S(2)}) copy-start(s32[512]{0:T(512)} %param.13) | copy-start | bytes 6148
  11.5 19.4 %copy-start.9 = (s32[32]{0:T(128)S(1)}, s32[32]{0:T(128)}, u32[]{:S(2)}) copy-start(s32[32]{0:T(128)} %param.12) | copy-start | bytes 388
  14.5 87.9 %collective-permute-start.7 = (bf16[2,352,256]{2,1,0:T(8,128)(2,1)}, bf16[2,352,256]{2,1,0:T(8,128)(2,1)S(1)}, u32[]{:S(2)}, u32[]{:S(2)}) collective-permute-start(bf16[2,352,256]{2,1,0:T(8,128)(2,1)} %get-tuple-element.60), channel_id=1, source_target_pairs={{4,0},{8,4},{12,8},{16,12},{20,16},{24,20},{28,24},{5,1},{9,5},{13... | collective-permute-start | bytes 1081352 | tf_op jit(solution)/shard_map/ppermute | solution.py:214
  15.8 73.8 %collective-permute-start.5 = (bf16[2,352,256]{2,1,0:T(8,128)(2,1)}, bf16[2,352,256]{2,1,0:T(8,128)(2,1)S(1)}, u32[]{:S(2)}, u32[]{:S(2)}) collective-permute-start(bf16[2,352,256]{2,1,0:T(8,128)(2,1)} %get-tuple-element.61), channel_id=1, source_target_pairs={{4,0},{8,4},{12,8},{16,12},{20,16},{24,20},{28,24},{5,1},{9,5},{13... | collective-permute-start | bytes 1081352 | tf_op jit(solution)/shard_map/ppermute | solution.py:214
  17.1 74.1 %collective-permute-start.4 = (bf16[2,352,256]{2,1,0:T(8,128)(2,1)S(1)}, bf16[2,352,256]{2,1,0:T(8,128)(2,1)S(1)}, u32[]{:S(2)}, u32[]{:S(2)}) collective-permute-start(bf16[2,352,256]{2,1,0:T(8,128)(2,1)S(1)} %get-tuple-element.62), channel_id=1, source_target_pairs={{0,4},{4,8},{8,12},{12,16},{16,20},{20,24},{24,28},{1,5},{5,9},{9,... | collective-permute-start | bytes 1081352 | tf_op jit(solution)/shard_map/ppermute | solution.py:213
  23.2 25.7 %collective-permute-start.1 = (bf16[2,352,256]{2,1,0:T(8,128)(2,1)S(1)}, bf16[2,352,256]{2,1,0:T(8,128)(2,1)S(1)}, u32[]{:S(2)}, u32[]{:S(2)}) collective-permute-start(bf16[2,352,256]{2,1,0:T(8,128)(2,1)S(1)} %get-tuple-element.65), channel_id=1, source_target_pairs={{4,0},{8,4},{12,8},{16,12},{20,16},{24,20},{28,24},{5,1},{9,5},{13... | collective-permute-start | bytes 1081352 | tf_op jit(solution)/shard_map/ppermute | solution.py:214
  24.5 34.6 %collective-permute-start = (bf16[2,352,256]{2,1,0:T(8,128)(2,1)}, bf16[2,352,256]{2,1,0:T(8,128)(2,1)S(1)}, u32[]{:S(2)}, u32[]{:S(2)}) collective-permute-start(bf16[2,352,256]{2,1,0:T(8,128)(2,1)} %get-tuple-element.66), channel_id=1, source_target_pairs={{0,4},{4,8},{8,12},{12,16},{16,20},{20,24},{24,28},{1,5},{5,9},{9,... | collective-permute-start | bytes 1081352 | tf_op jit(solution)/shard_map/ppermute | solution.py:213
  43.6 2.2 %copy-start.1 = (bf16[3,352,2048]{2,1,0:T(8,128)(2,1)S(1)}, bf16[3,352,2048]{2,1,0:T(8,128)(2,1)}, u32[]{:S(2)}) copy-start(bf16[3,352,2048]{2,1,0:T(8,128)(2,1)} %qkv_ref.1) | copy-start | bytes 12976132
  45.8 3.2 %copy-start.6 = (bf16[2,352,256]{2,1,0:T(8,128)(2,1)S(1)}, bf16[2,352,256]{2,1,0:T(8,128)(2,1)}, u32[]{:S(2)}) copy-start(bf16[2,352,256]{2,1,0:T(8,128)(2,1)} %get-tuple-element.63) | copy-start | bytes 1081348
  47.6 1.4 copy-start.5
  49.0 23.6 %copy-start.4 = (bf16[8,4,128,256]{3,2,1,0:T(8,128)(2,1)}, bf16[8,4,128,256]{3,2,1,0:T(8,128)(2,1)S(1)}, u32[]{:S(2)}) copy-start(bf16[8,4,128,256]{3,2,1,0:T(8,128)(2,1)S(1)} %get-tuple-element.29.q_low.q_high) | copy-start | bytes 6291460
  49.0 23.6 %collective-permute-start.3 = (bf16[2,352,256]{2,1,0:T(8,128)(2,1)S(1)}, bf16[2,352,256]{2,1,0:T(8,128)(2,1)S(1)}, u32[]{:S(2)}, u32[]{:S(2)}) collective-permute-start(bf16[2,352,256]{2,1,0:T(8,128)(2,1)S(1)} %copy-done.6), channel_id=1, source_target_pairs={{4,0},{8,4},{12,8},{16,12},{20,16},{24,20},{28,24},{5,1},{9,5},{13... | collective-permute-start | bytes 1081352 | tf_op jit(solution)/shard_map/ppermute | solution.py:214
  59.1 18.0 %collective-permute-start.2 = (bf16[2,352,256]{2,1,0:T(8,128)(2,1)S(1)}, bf16[2,352,256]{2,1,0:T(8,128)(2,1)S(1)}, u32[]{:S(2)}, u32[]{:S(2)}) collective-permute-start(bf16[2,352,256]{2,1,0:T(8,128)(2,1)S(1)} %get-tuple-element.64), channel_id=1, source_target_pairs={{0,4},{4,8},{8,12},{12,16},{16,20},{20,24},{24,28},{1,5},{5,9},{9,... | collective-permute-start | bytes 1081352 | tf_op jit(solution)/shard_map/ppermute | solution.py:213
  72.6 30.4 %collective-permute-start.6 = (bf16[2,352,256]{2,1,0:T(8,128)(2,1)}, bf16[2,352,256]{2,1,0:T(8,128)(2,1)S(1)}, u32[]{:S(2)}, u32[]{:S(2)}) collective-permute-start(bf16[2,352,256]{2,1,0:T(8,128)(2,1)} %get-tuple-element.67), channel_id=1, source_target_pairs={{0,4},{4,8},{8,12},{12,16},{16,20},{20,24},{24,28},{1,5},{5,9},{9,... | collective-permute-start | bytes 1081352 | tf_op jit(solution)/shard_map/ppermute | solution.py:213
  77.1 37.1 %collective-permute-start.18 = (bf16[352,512]{1,0:T(8,128)(2,1)S(1)}, bf16[352,512]{1,0:T(8,128)(2,1)S(1)}, u32[]{:S(2)}, u32[]{:S(2)}) collective-permute-start(bf16[352,512]{1,0:T(8,128)(2,1)S(1)} %attend.7.refs_0_), channel_id=1, source_target_pairs={{0,1},{1,0},{2,3},{3,2},{4,5},{5,4},{6,7},{7,6},{8,9},{9,8},{10,11... | collective-permute-start | bytes 1081352 | tf_op jit(solution)/shard_map/ppermute | solution.py:360
  89.6 15.1 %collective-permute-start.17 = (bf16[352,512]{1,0:T(8,128)(2,1)S(1)}, bf16[352,512]{1,0:T(8,128)(2,1)S(1)}, u32[]{:S(2)}, u32[]{:S(2)}) collective-permute-start(bf16[352,512]{1,0:T(8,128)(2,1)S(1)} %attend.7.refs_0_), channel_id=1, source_target_pairs={{0,2},{1,3},{2,0},{3,1},{4,6},{5,7},{6,4},{7,5},{8,10},{9,11},{10,... | collective-permute-start | bytes 1081352 | tf_op jit(solution)/shard_map/ppermute | solution.py:360
  91.2 40.2 %collective-permute-start.15 = (bf16[352,512]{1,0:T(8,128)(2,1)S(1)}, bf16[352,512]{1,0:T(8,128)(2,1)S(1)}, u32[]{:S(2)}, u32[]{:S(2)}) collective-permute-start(bf16[352,512]{1,0:T(8,128)(2,1)S(1)} %attend.6.refs_0_), channel_id=1, source_target_pairs={{0,1},{1,0},{2,3},{3,2},{4,5},{5,4},{6,7},{7,6},{8,9},{9,8},{10,11... | collective-permute-start | bytes 1081352 | tf_op jit(solution)/shard_map/ppermute | solution.py:360
  102.4 12.4 %collective-permute-start.14 = (bf16[352,512]{1,0:T(8,128)(2,1)S(1)}, bf16[352,512]{1,0:T(8,128)(2,1)}, u32[]{:S(2)}, u32[]{:S(2)}) collective-permute-start(bf16[352,512]{1,0:T(8,128)(2,1)S(1)} %attend.6.refs_0_), channel_id=1, source_target_pairs={{0,2},{1,3},{2,0},{3,1},{4,6},{5,7},{6,4},{7,5},{8,10},{9,11},{10,... | collective-permute-start | bytes 1081352 | tf_op jit(solution)/shard_map/ppermute | solution.py:360
  103.0 18.6 %collective-permute-start.11 = (bf16[352,512]{1,0:T(8,128)(2,1)S(1)}, bf16[352,512]{1,0:T(8,128)(2,1)}, u32[]{:S(2)}, u32[]{:S(2)}) collective-permute-start(bf16[352,512]{1,0:T(8,128)(2,1)S(1)} %attend.5.refs_0_), channel_id=1, source_target_pairs={{0,2},{1,3},{2,0},{3,1},{4,6},{5,7},{6,4},{7,5},{8,10},{9,11},{10,... | collective-permute-start | bytes 1081352 | tf_op jit(solution)/shard_map/ppermute | solution.py:360
  104.8 9.5 %copy-start.2 = (bf16[352,512]{1,0:T(8,128)(2,1)}, bf16[352,512]{1,0:T(8,128)(2,1)S(1)}, u32[]{:S(2)}) copy-start(bf16[352,512]{1,0:T(8,128)(2,1)S(1)} %collective-permute-done.17.refs_1_) | copy-start | bytes 1081348
  104.8 17.2 %collective-permute-start.19 = (bf16[352,512]{1,0:T(8,128)(2,1)S(1)}, bf16[352,512]{1,0:T(8,128)(2,1)}, u32[]{:S(2)}, u32[]{:S(2)}) collective-permute-start(bf16[352,512]{1,0:T(8,128)(2,1)S(1)} %collective-permute-done.17.refs_1_), channel_id=1, source_target_pairs={{0,1},{1,0},{2,3},{3,2},{4,5},{5,4},{6,7},{7,6},{8,9},{9,8},{10,11... | collective-permute-start | bytes 1081352 | tf_op jit(solution)/shard_map/ppermute | solution.py:360
  104.8 10.2 %copy-start.7 = (f32[1408]{0:T(1024)S(1)}, f32[1408]{0:T(1024)}, u32[]{:S(2)}) copy-start(f32[1408]{0:T(1024)} %param.11) | copy-start | bytes 16900
  114.2 17.6 %collective-permute-start.8 = (bf16[352,512]{1,0:T(8,128)(2,1)}, bf16[352,512]{1,0:T(8,128)(2,1)}, u32[]{:S(2)}, u32[]{:S(2)}) collective-permute-start(bf16[352,512]{1,0:T(8,128)(2,1)} %attend.4.refs_0_), channel_id=1, source_target_pairs={{0,2},{1,3},{2,0},{3,1},{4,6},{5,7},{6,4},{7,5},{8,10},{9,11},{10,... | collective-permute-start | bytes 1081352 | tf_op jit(solution)/shard_map/ppermute | solution.py:360
  114.8 17.2 %collective-permute-start.16 = (bf16[352,512]{1,0:T(8,128)(2,1)}, bf16[352,512]{1,0:T(8,128)(2,1)}, u32[]{:S(2)}, u32[]{:S(2)}) collective-permute-start(bf16[352,512]{1,0:T(8,128)(2,1)} %collective-permute-done.14.refs_1_), channel_id=1, source_target_pairs={{0,1},{1,0},{2,3},{3,2},{4,5},{5,4},{6,7},{7,6},{8,9},{9,8},{10,11... | collective-permute-start | bytes 1081352 | tf_op jit(solution)/shard_map/ppermute | solution.py:360
  121.6 18.8 %collective-permute-start.12 = (bf16[352,512]{1,0:T(8,128)(2,1)S(1)}, bf16[352,512]{1,0:T(8,128)(2,1)}, u32[]{:S(2)}, u32[]{:S(2)}) collective-permute-start(bf16[352,512]{1,0:T(8,128)(2,1)S(1)} %attend.5.refs_0_), channel_id=1, source_target_pairs={{0,1},{1,0},{2,3},{3,2},{4,5},{5,4},{6,7},{7,6},{8,9},{9,8},{10,11... | collective-permute-start | bytes 1081352 | tf_op jit(solution)/shard_map/ppermute | solution.py:360
  122.0 18.4 %collective-permute-start.13 = (bf16[352,512]{1,0:T(8,128)(2,1)}, bf16[352,512]{1,0:T(8,128)(2,1)}, u32[]{:S(2)}, u32[]{:S(2)}) collective-permute-start(bf16[352,512]{1,0:T(8,128)(2,1)} %collective-permute-done.11.refs_1_), channel_id=1, source_target_pairs={{0,1},{1,0},{2,3},{3,2},{4,5},{5,4},{6,7},{7,6},{8,9},{9,8},{10,11... | collective-permute-start | bytes 1081352 | tf_op jit(solution)/shard_map/ppermute | solution.py:360
  122.1 1.0 copy-start.3
  131.4 17.4 %collective-permute-start.9 = (bf16[352,512]{1,0:T(8,128)(2,1)}, bf16[352,512]{1,0:T(8,128)(2,1)S(1)}, u32[]{:S(2)}, u32[]{:S(2)}) collective-permute-start(bf16[352,512]{1,0:T(8,128)(2,1)} %attend.4.refs_0_), channel_id=1, source_target_pairs={{0,1},{1,0},{2,3},{3,2},{4,5},{5,4},{6,7},{7,6},{8,9},{9,8},{10,11... | collective-permute-start | bytes 1081352 | tf_op jit(solution)/shard_map/ppermute | solution.py:360
  131.8 17.0 %collective-permute-start.10 = (bf16[352,512]{1,0:T(8,128)(2,1)}, bf16[352,512]{1,0:T(8,128)(2,1)S(1)}, u32[]{:S(2)}, u32[]{:S(2)}) collective-permute-start(bf16[352,512]{1,0:T(8,128)(2,1)} %collective-permute-done.8.refs_1_), channel_id=1, source_target_pairs={{0,1},{1,0},{2,3},{3,2},{4,5},{5,4},{6,7},{7,6},{8,9},{9,8},{10,11... | collective-permute-start | bytes 1081352 | tf_op jit(solution)/shard_map/ppermute | solution.py:360
  158.7 23.6 %all-to-all-start = ((bf16[8,64,384]{2,1,0:T(8,128)(2,1)}), bf16[8,64,384]{2,1,0:T(8,128)(2,1)S(1)}, u32[]{:S(2)}, u32[]{:S(2)}) async-start(bf16[8,64,384]{2,1,0:T(8,128)(2,1)} %bitcast.27), calls=%async_computation | async-start | bytes 786432 | tf_op jit(solution)/shard_map/all_to_all | solution.py:433
Sparse Core Ops, SparseCore 0:
  11.6 46.0 all-gather.2
